TPU v7x, 32 devices: a whole 2x2x4 slice. The times are simulated.
32 devices in a mesh: ctx: 8 (over y, x, core), tp: 4 (over z).
Axes of the slice: x: 2, y: 2, z: 4, core: 2. Of those that a mesh axis runs over, the one named last changes fastest.
Arguments:
- gate_input: bfloat16 [2048, 8192], P('ctx', 'tp'), may hold values from -6 to 6
- value_input: bfloat16 [2048, 8192], P('ctx', 'tp'), may hold values from -6 to 6
- filter_taps: float32 [2048, 8192], P('ctx', 'tp'), may hold values from -1 to 1
- skip_gain: float32 [8192], P('tp'), may hold values from 0.3 to 3
- queries: bfloat16 [2048, 8192], P('ctx', 'tp'), may hold values from -8 to 8
- keys: bfloat16 [2048, 8192], P('ctx', 'tp'), may hold values from -8 to 8
Outputs:
- mixed: bfloat16 [2048, 8192], P('ctx', 'tp')
- attended: bfloat16 [2048, 8192], P('ctx', 'tp')
All inputs are finite; a program needn't handle non-finite values.
Results may differ from a plain program's by a relative error of at most 0.012.
Values may be sent and summed in bfloat16 or wider, within the bound.
A program may use at most 128 MiB of HBM per device.

v0:
```python
import math

import jax
import jax.numpy as jnp
from jax import lax
from jax.sharding import PartitionSpec as P

HEAD_DIM = 128


PRECISE = lax.Precision.HIGHEST
TWO_PI = 2.0 * math.pi


def as_sent(value):

    def short(part):
        return part.astype(jnp.bfloat16) if part.dtype == jnp.float32 else part

    return jax.tree.map(short, value)


def unit_roots(first_index, second_index, period, orient):
    product = first_index[:, None] * second_index[None, :] % period
    angles = TWO_PI / period * product.astype(jnp.float32)
    return (jnp.cos(angles), orient * jnp.sin(angles))


def first_section(signal, shards):
    cosine, sine_part = unit_roots(
        jnp.arange(2 * shards, dtype=jnp.int32),
        jnp.arange(shards, dtype=jnp.int32),
        2 * shards,
        -1.0,
    )
    real_part = jnp.einsum("kn,nmc->kmc", cosine, signal, precision=PRECISE)
    imag_part = jnp.einsum("kn,nmc->kmc", sine_part, signal, precision=PRECISE)
    return (real_part, imag_part)


def twist(real_part, imag_part, outer_index, inner_index, padded, orient):
    cosine, sine_part = unit_roots(outer_index, inner_index, padded, orient)
    cosine = cosine[:, :, None]
    sine_part = sine_part[:, :, None]
    return (real_part * cosine - imag_part * sine_part, real_part * sine_part + imag_part * cosine)


def contract(matrix, operand):
    return jnp.einsum("qn,knc->kqc", matrix, operand, precision=PRECISE)


def second_section(real_part, imag_part, orient):
    length = real_part.shape[1]
    indices = jnp.arange(length, dtype=jnp.int32)
    cosine, sine_part = unit_roots(indices, indices, length, orient)
    new_real = contract(cosine, real_part) - contract(sine_part, imag_part)
    new_imag = contract(sine_part, real_part) + contract(cosine, imag_part)
    return (new_real, new_imag)


def last_section(real_part, imag_part, shards, padded):
    cosine, sine_part = unit_roots(
        jnp.arange(shards, dtype=jnp.int32),
        jnp.arange(2 * shards, dtype=jnp.int32),
        2 * shards,
        1.0,
    )
    summed = jnp.einsum("nk,kmc->nmc", cosine, real_part, precision=PRECISE) - jnp.einsum(
        "nk,kmc->nmc", sine_part, imag_part, precision=PRECISE
    )
    return summed * (1.0 / padded)


def spectral_product(signal_spectrum, filter_spectrum):
    signal_real, signal_imag = signal_spectrum
    filter_real, filter_imag = filter_spectrum
    return (
        signal_real * filter_real - signal_imag * filter_imag,
        signal_real * filter_imag + signal_imag * filter_real,
    )


def per_device(gate_input, value_input, filter_taps, skip_gain, queries, keys):
    shards = lax.axis_size("ctx")
    my_index = lax.axis_index("ctx")
    tok_rows, channels = value_input.shape
    padded = 2 * shards * tok_rows
    signal = value_input.astype(jnp.float32)
    wide_index = jnp.arange(2 * shards, dtype=jnp.int32)
    slab_rows = tok_rows // shards
    moved_signal, moved_taps = (
        lax.all_to_all(
            signal.reshape(1, tok_rows, channels).astype(jnp.bfloat16),
            "ctx",
            split_axis=1,
            concat_axis=0,
            tiled=True,
        ).astype(jnp.float32),
        lax.all_to_all(
            filter_taps.reshape(1, tok_rows, channels).astype(jnp.bfloat16),
            "ctx",
            split_axis=1,
            concat_axis=0,
            tiled=True,
        ).astype(jnp.float32),
    )
    inner_index = my_index * slab_rows + jnp.arange(slab_rows, dtype=jnp.int32)

    def spread_front(block):
        real_part, imag_part = first_section(block, shards)
        real_part, imag_part = twist(real_part, imag_part, wide_index, inner_index, padded, -1.0)
        return jnp.stack([real_part, imag_part])

    turned_signal, turned_taps = (
        lax.all_to_all(
            as_sent(spread_front(moved_signal)), "ctx", split_axis=1, concat_axis=2, tiled=True
        ),
        lax.all_to_all(
            as_sent(spread_front(moved_taps)), "ctx", split_axis=1, concat_axis=2, tiled=True
        ),
    )
    signal_spectrum = second_section(turned_signal[0], turned_signal[1], -1.0)
    filter_spectrum = second_section(turned_taps[0], turned_taps[1], -1.0)
    real_part, imag_part = spectral_product(signal_spectrum, filter_spectrum)
    real_part, imag_part = second_section(real_part, imag_part, 1.0)
    outer_index = 2 * my_index + jnp.arange(2, dtype=jnp.int32)
    real_part, imag_part = twist(
        real_part, imag_part, outer_index, jnp.arange(tok_rows, dtype=jnp.int32), padded, 1.0
    )
    returned = lax.all_to_all(
        as_sent(jnp.stack([real_part, imag_part])), "ctx", split_axis=2, concat_axis=1, tiled=True
    )
    blocks = last_section(returned[0], returned[1], shards, padded)
    convolved = (
        lax.all_to_all(as_sent(blocks), "ctx", split_axis=0, concat_axis=1, tiled=True)
        .astype(blocks.dtype)
        .reshape(tok_rows, channels)
    )
    mixed = (gate_input.astype(jnp.float32) * (convolved + skip_gain[None, :] * signal)).astype(
        jnp.bfloat16
    )
    head_count = channels // HEAD_DIM
    scale_factor = 1.0 / math.sqrt(HEAD_DIM)
    query_heads = queries.reshape(tok_rows, head_count, HEAD_DIM)
    query_pos = my_index * tok_rows + jnp.arange(tok_rows, dtype=jnp.int32)
    running_max = jnp.full((head_count, tok_rows), -1e30, jnp.float32)
    key_block = lax.all_gather(keys, "ctx", axis=0, tiled=True)
    value_block = lax.all_gather(mixed, "ctx", axis=0, tiled=True)
    key_rows = key_block.shape[0]
    key_heads = key_block.reshape(key_rows, head_count, HEAD_DIM)
    value_heads = value_block.reshape(key_rows, head_count, HEAD_DIM)
    scores = (
        jnp.einsum("qhd,khd->hqk", query_heads, key_heads, preferred_element_type=jnp.float32)
        * scale_factor
    )
    key_pos = jnp.arange(key_rows, dtype=jnp.int32)
    allowed = (key_pos[None, :] <= query_pos[:, None])[None]
    masked = jnp.where(allowed, scores, -1e30)
    newest = jnp.maximum(running_max, jnp.max(masked, axis=2))
    weights = jnp.where(allowed, jnp.exp(masked - newest[:, :, None]), 0.0)
    total_weight = jnp.sum(weights, axis=2)
    update = jnp.einsum(
        "hqk,khd->hqd",
        weights.astype(jnp.bfloat16),
        value_heads,
        preferred_element_type=jnp.float32,
    )
    accumulated = update
    running_max, total_weight, accumulated = (newest, total_weight, accumulated)
    attended = (
        (accumulated / total_weight[:, :, None])
        .transpose(1, 0, 2)
        .reshape(tok_rows, channels)
        .astype(jnp.bfloat16)
    )
    return (mixed, attended)


def solution(mesh):
    placed = (
        P("ctx", "tp"),
        P("ctx", "tp"),
        P("ctx", "tp"),
        P("tp"),
        P("ctx", "tp"),
        P("ctx", "tp"),
    )
    return jax.shard_map(
        per_device,
        mesh=mesh,
        in_specs=placed,
        out_specs=(P("ctx", "tp"), P("ctx", "tp")),
        check_vma=False,
    )
```

profile of v0, /device:TPU:0, one launch (start us, length us, event | category | flops | bytes accessed | tf_op | source)
XLA Modules:
  0.0 460.3 jit_solution(2343517530670462375)
XLA Ops:
  11.2 7.8 %reduce = bf16[256,2048]{1,0:T(8,128)(2,1)} reduce(bf16[256,1,2048]{2,1,0:T(2,128)(2,1)S(1)} %bitcast.162, bf16[]{:T(256)} %broadcast.394), dimensions={1}, to_apply=%bitcast.141.reduce_sub_computation | reduce | bytes 2097154
  21.5 5.4 %all-to-all-start.2 = ((bf16[8,2,32768]{2,1,0:T(2,128)(2,1)}), bf16[8,2,32768]{2,1,0:T(2,128)(2,1)}, u32[]{:S(2)}, u32[]{:S(2)}) async-start(bf16[8,2,32768]{2,1,0:T(2,128)(2,1)} %reshape.201), calls=%async_computation.2 | async-start | bytes 2097152 | tf_op jit(solution)/shard_map/all_to_all | solution.py:99
  29.8 7.8 %reduce.1 = bf16[256,2048]{1,0:T(8,128)(2,1)} reduce(bf16[256,1,2048]{2,1,0:T(2,128)(2,1)S(1)} %bitcast.163, bf16[]{:T(256)} %broadcast.394), dimensions={1}, to_apply=%bitcast.142.reduce_sub_computation | reduce | bytes 2097154
  42.4 4.6 %all-to-all-start = ((bf16[8,2,32768]{2,1,0:T(2,128)(2,1)}), bf16[8,2,32768]{2,1,0:T(2,128)(2,1)}, u32[]{:S(2)}, u32[]{:S(2)}) async-start(bf16[8,2,32768]{2,1,0:T(2,128)(2,1)} %reshape.199), calls=%async_computation | async-start | bytes 2097152 | tf_op jit(solution)/shard_map/all_to_all | solution.py:92
  47.3 4.3 reshape.202
  52.2 3.6 fusion.36
  55.8 3.6 fusion.38
  62.5 4.3 reshape.200
  70.3 5.1 %fusion.24 = (bf16[1,16,32,2048]{3,1,2,0:T(8,128)(2,1)S(1)}, bf16[1,16,32,2048]{3,1,2,0:T(8,128)(2,1)S(1)}, bf16[1,16,32,2048]{3,1,2,0:T(8,128)(2,1)S(1)}, bf16[1,16,32,2048]{3,1,2,0:T(8,128)(2,1)}) fusion(f32[16,32,2048]{2,0,1:T(8,128)S(1)} %copy-done.2, f32[16,32,2048]{2,0,1:T(8,128)S(1)} %copy-done.3, f32[16,32]{0,1:T(8,128)S(1)} %get-tuple-element.29, ...), kind=kOutput, calls=%fused_computation.37 | convolution fusion | flops 117442304 | bytes 22024192 | tf_op jit(solution)/shard_map/kn,nmc->kmc/dot_general | solution.py:36
  75.8 4.3 copy.76
  80.1 4.6 all-to-all-start.3
  86.6 4.3 copy.67
  90.9 42.9 %all-to-all-done.3 = bf16[2,16,32,2048]{3,2,0,1:T(8,128)(2,1)} async-done(((bf16[2,16,32,2048]{3,2,0,1:T(8,128)(2,1)}), bf16[2,16,32,2048]{3,2,0,1:T(8,128)(2,1)}, u32[]{:S(2)}, u32[]{:S(2)}) %all-to-all-start.3) | async-done | bytes 4194336 | tf_op jit(solution)/shard_map/all_to_all | solution.py:118
  133.8 4.6 all-to-all-start.1
  144.9 55.7 %all-to-all-done.1 = bf16[2,16,32,2048]{3,2,0,1:T(8,128)(2,1)} async-done(((bf16[2,16,32,2048]{3,2,0,1:T(8,128)(2,1)}), bf16[2,16,32,2048]{3,2,0,1:T(8,128)(2,1)}, u32[]{:S(2)}, u32[]{:S(2)}) %all-to-all-start.1) | async-done | bytes 4194336 | tf_op jit(solution)/shard_map/all_to_all | solution.py:115
  212.0 5.4 %fusion.51 = f32[2,2048,256]{2,1,0:T(8,128)} fusion(bf16[2,256,2048]{2,1,0:T(8,128)(2,1)S(1)} %bitcast.147), kind=kOutput, calls=%fused_computation.69 | convolution fusion | flops 3222208512 | bytes 6291456 | tf_op jit(solution)/shard_map/qn,knc->kqc/dot_general | solution.py:49
  227.9 4.0 convolution_subtract_fusion.1
  231.9 6.4 %multiply_subtract_fusion = (f32[2,2048,256]{2,1,0:T(8,128)S(1)}, f32[2,2048,256]{2,1,0:T(8,128)S(1)}) fusion(f32[2,2048,256]{2,1,0:T(8,128)S(1)} %convolution_add_fusion, f32[2,2048,256]{2,1,0:T(8,128)S(1)} %convolution_subtract_fusion.1, f32[2,2048,256]{2,1,0:T(8,128)S(1)} %convolution_subtract_fusion, f32[2,2048,256]{2,1,0:T(8,128)} %fusion.51, ...), kind=kOutput, calls=%fused_computation.21 | convolution fusion | flops 3229483008 | bytes 27262976 | tf_op jit(solution)/shard_map/qn,knc->kqc/dot_general | solution.py:49
  238.3 4.6 fusion.6
  242.9 4.6 fusion.8
  247.5 4.4 fusion.14
  251.9 5.6 %fusion.26 = (bf16[1,2,256,2048]{2,3,1,0:T(8,128)(2,1)S(1)}, bf16[1,2,256,2048]{2,3,1,0:T(8,128)(2,1)S(1)}) fusion(f32[2,2048,256]{2,1,0:T(8,128)S(1)} %fusion.14, f32[2,256]{1,0:T(2,128)S(1)} %get-tuple-element.27, f32[2,256]{1,0:T(2,128)S(1)} %get-tuple-element.26, f32[2,2048,256]{2,1,0:T(8,128)S(1)} %fusion.6, f32[2,2048,256]{2,1,0:T(8,128)S(1)} %get-tuple-element.10), kind=kOutput, calls=%fused_computation.39 | convolution fusion | flops 3231580160 | bytes 16781312 | tf_op jit(solution)/shard_map/qn,knc->kqc/dot_general | solution.py:49
  259.8 11.2 %copy.86 = bf16[2,2,256,2048]{3,1,0,2:T(2,128)(2,1)} copy(bf16[2,2,256,2048]{2,3,1,0:T(8,128)(2,1)} %pad_maximum_fusion.2) | data formatting | bytes 8388608 | tf_op jit(solution)/shard_map/stack | solution.py:131
  271.0 52.7 %all_to_all.78 = bf16[2,2,256,2048]{3,1,0,2:T(2,128)(2,1)S(1)} all-to-all(bf16[2,2,256,2048]{3,1,0,2:T(2,128)(2,1)} %copy.86), channel_id=1, replica_groups=mesh['ctx'=8,'tp'=4] {'ctx'}, dimensions={2} | all-to-all | bytes 8388608 | tf_op jit(solution)/shard_map/all_to_all | solution.py:130
  334.0 5.1 %copy.88 = bf16[1,8,2,32,2048]{4,2,1,3,0:T(2,128)(2,1)} copy(bf16[1,8,2,32,2048]{4,3,1,2,0:T(8,128)(2,1)} %get-tuple-element.19) | data formatting | bytes 4194304 | tf_op jit(solution)/shard_map/slice | solution.py:133
  339.1 4.1 squeeze.22
  347.6 18.0 %all_to_all.79 = bf16[8,32,2048]{2,1,0:T(8,128)(2,1)S(1)} all-to-all(bf16[8,32,2048]{2,1,0:T(8,128)(2,1)S(1)} %copy.90), channel_id=1, replica_groups=mesh['ctx'=8,'tp'=4] {'ctx'}, dimensions={0} | all-to-all | bytes 2097152 | tf_op jit(solution)/shard_map/all_to_all | solution.py:135
  367.7 18.4 %fusion = (f32[16,256]{1,0:T(8,128)S(1)}, f32[16,256,2048]{2,1,0:T(8,128)}) fusion(pred[256,2048]{1,0:T(8,128)(4,1)S(1)} %iota_compare_fusion, bf16[2048,16,128]{0,2,1:T(8,128)(2,1)} %bitcast.151, bf16[256,2048]{1,0:T(8,128)(2,1)S(1)} %copy-done), kind=kOutput, calls=%fused_computation.2 | convolution fusion | flops 2172645376 | bytes 43532288 | tf_op jit(solution)/shard_map/qhd,khd->hqk/dot_general | solution.py:153
  386.1 16.4 %fusion.1 = f32[16,256]{1,0:T(8,128)S(1)} fusion(f32[16,256,2048]{2,1,0:T(8,128)} %get-tuple-element.31, f32[16,256]{1,0:T(8,128)S(1)} %broadcast_maximum_fusion, pred[256,2048]{1,0:T(8,128)(4,1)S(1)} %iota_compare_fusion), kind=kLoop, calls=%fused_computation.3 | loop fusion | flops 41938944 | bytes 34111488 | tf_op jit(solution)/shard_map/reduce_sum | solution.py:161
  402.5 19.7 %all-gather.5.cloned.1.call-done = bf16[2048,2048]{1,0:T(8,128)(2,1)} async-done(((bf16[256,2048]{1,0:T(8,128)(2,1)}), bf16[2048,2048]{1,0:T(8,128)(2,1)}) %all-gather.5.cloned.1.call-update) | async-done | bytes 8388624 | tf_op jit(solution)/shard_map/all_gather | solution.py:148
  422.3 12.3 %copy.94 = bf16[2048,2048]{0,1:T(8,128)(2,1)} copy(bf16[2048,2048]{1,0:T(8,128)(2,1)} %all-gather.5.cloned.1.call-done) | data formatting | bytes 16777216 | tf_op jit(solution)/shard_map/all_gather | solution.py:148
  434.6 17.0 %fusion.30 = bf16[256,16,128]{0,2,1:T(8,128)(2,1)S(1)} fusion(bf16[2048,16,128]{0,2,1:T(8,128)(2,1)} %bitcast.161, f32[16,256,2048]{2,1,0:T(8,128)} %get-tuple-element.31, f32[16,256]{1,0:T(8,128)S(1)} %broadcast_maximum_fusion, pred[256,2048]{1,0:T(8,128)(4,1)S(1)} %iota_compare_fusion, f32[256,16]{0,1:T(8,128)S(1)} %bitcast.166), kind=kOutput, calls=%fused_computation.45 | convolution fusion | flops 2190475264 | bytes 43548672 | tf_op jit(solution)/shard_map/hqk,khd->hqd/dot_general | solution.py:162
  (65 shorter events, 72.7 us)
Async XLA Ops:
  7.2 360.5 %copy-start = (bf16[256,2048]{1,0:T(8,128)(2,1)S(1)}, bf16[256,2048]{1,0:T(8,128)(2,1)}, u32[]{:S(2)}) copy-start(bf16[256,2048]{1,0:T(8,128)(2,1)} %param.10) | copy-start | bytes 3145732
  21.5 20.9 %all-to-all-start.2 = ((bf16[8,2,32768]{2,1,0:T(2,128)(2,1)}), bf16[8,2,32768]{2,1,0:T(2,128)(2,1)}, u32[]{:S(2)}, u32[]{:S(2)}) async-start(bf16[8,2,32768]{2,1,0:T(2,128)(2,1)} %reshape.201), calls=%async_computation.2 | async-start | bytes 2097152 | tf_op jit(solution)/shard_map/all_to_all | solution.py:99
  42.4 20.1 %all-to-all-start = ((bf16[8,2,32768]{2,1,0:T(2,128)(2,1)}), bf16[8,2,32768]{2,1,0:T(2,128)(2,1)}, u32[]{:S(2)}, u32[]{:S(2)}) async-start(bf16[8,2,32768]{2,1,0:T(2,128)(2,1)} %reshape.199), calls=%async_computation | async-start | bytes 2097152 | tf_op jit(solution)/shard_map/all_to_all | solution.py:92
  66.8 2.8 copy-start.2
  66.8 3.5 copy-start.3
  80.1 53.7 %all-to-all-start.3 = ((bf16[2,16,32,2048]{3,2,0,1:T(8,128)(2,1)}), bf16[2,16,32,2048]{3,2,0,1:T(8,128)(2,1)}, u32[]{:S(2)}, u32[]{:S(2)}) async-start(bf16[2,16,32,2048]{3,2,0,1:T(8,128)(2,1)} %copy.76), calls=%async_computation.3 | async-start | bytes 8388608 | tf_op jit(solution)/shard_map/all_to_all | solution.py:118
  90.9 47.5 %copy-start.5 = (bf16[256,2048]{1,0:T(8,128)(2,1)S(1)}, bf16[256,2048]{1,0:T(8,128)(2,1)}, u32[]{:S(2)}) copy-start(bf16[256,2048]{1,0:T(8,128)(2,1)} %param.11) | copy-start | bytes 3145732
  133.8 66.8 %all-to-all-start.1 = ((bf16[2,16,32,2048]{3,2,0,1:T(8,128)(2,1)}), bf16[2,16,32,2048]{3,2,0,1:T(8,128)(2,1)}, u32[]{:S(2)}, u32[]{:S(2)}) async-start(bf16[2,16,32,2048]{3,2,0,1:T(8,128)(2,1)} %copy.67), calls=%async_computation.1 | async-start | bytes 8388608 | tf_op jit(solution)/shard_map/all_to_all | solution.py:115
  138.4 229.3 %all-gather.3.cloned.1.call-start = ((), (), s32[]{:S(2)}) async-start(), calls=%async_computation.6 | async-start | bytes 9437184 | tf_op jit(solution)/shard_map/all_gather | solution.py:147
  139.8 282.5 %all-gather.5.cloned.1.call-start = ((), (), s32[]{:S(2)}) async-start(), calls=%async_computation.7 | async-start | bytes 9437184 | tf_op jit(solution)/shard_map/all_gather | solution.py:148
  203.5 1.6 copy-start.1
  345.8 19.9 %copy-start.4 = (bf16[256,2048]{1,0:T(8,128)(2,1)S(1)}, bf16[256,2048]{1,0:T(8,128)(2,1)}, u32[]{:S(2)}) copy-start(bf16[256,2048]{1,0:T(8,128)(2,1)} %param.7) | copy-start | bytes 3145732
  345.8 19.8 %copy-start.6 = (bf16[256,2048]{1,0:T(8,128)(2,1)S(1)}, bf16[256,2048]{1,0:T(8,128)(2,1)}, u32[]{:S(2)}) copy-start(bf16[256,2048]{1,0:T(8,128)(2,1)} %param.6) | copy-start | bytes 3145732
  345.8 19.8 %copy-start.7 = (f32[2048]{0:T(1024)S(1)}, f32[2048]{0:T(1024)}, u32[]{:S(2)}) copy-start(f32[2048]{0:T(1024)} %param.9) | copy-start | bytes 24580
Sparse Core Ops, SparseCore 0:
  141.7 83.0 all-gather.2
  367.4 54.7 all-gather.4
where the time goes:
time: 469 us; the launch traced here: 460 us
  waiting for transfers between devices  124 us (26%)
  matrix products  106 us (23%)
  local copies, waits for them, and re-layouts  85 us (18%)
  blocking collectives  70.7 us (15%)
  other arithmetic  40.6 us (9%)
  starting transfers between devices  19.5 us (4%)
  between operations  14.9 us (3%)
    all_to_all x1, waiting for transfers between devices, per_device(): lax.all_to_all(as_sent(spread_front(moved_signal)), 'ctx', split_axis=1,...  55.7 us
    all_to_all x1, blocking collectives, per_device(): lax.all_to_all(as_sent(jnp.stack([real_part, imag_part])), 'ctx', split_a...  52.7 us
    dot_general x12, matrix products, contract(): return jnp.einsum('qn,knc->kqc', matrix, operand, precision=PRECISE)  52.2 us
    all_to_all x1, waiting for transfers between devices, per_device(): lax.all_to_all(as_sent(spread_front(moved_taps)), 'ctx', split_axis=1, co...  42.9 us
    unnamed x25, local copies, waits for them, and re-layouts  20.3 us
    all_gather x1, waiting for transfers between devices, per_device(): value_block = lax.all_gather(mixed, 'ctx', axis=0, tiled=True)  19.7 us
    dot_general x1, matrix products, per_device(): jnp.einsum('qhd,khd->hqk', query_heads, key_heads, preferred_element_type...  18.4 us
    all_to_all x1, blocking collectives, per_device(): lax.all_to_all(as_sent(blocks), 'ctx', split_axis=0, concat_axis=1, tiled...  18 us
  transfers between devices with their start and end apart: 6, of which 5 were waited for; matrix products, arithmetic and copies ran while one was open for 36% of the time, Pallas kernels for 0%

commit v1 on v0

--- a/solution.py
+++ b/solution.py
@@ -1,8 +1,12 @@
+import functools
 import math
 
 import jax
 import jax.numpy as jnp
+import numpy as np
 from jax import lax
+from jax.experimental import pallas as pl
+from jax.experimental.pallas import tpu as pltpu
 from jax.sharding import PartitionSpec as P
 
 HEAD_DIM = 128
@@ -80,7 +84,7 @@
     )
 
 
-def per_device(gate_input, value_input, filter_taps, skip_gain, queries, keys):
+def by_sequence(gate_input, value_input, filter_taps, skip_gain, queries, keys):
     shards = lax.axis_size("ctx")
     my_index = lax.axis_index("ctx")
     tok_rows, channels = value_input.shape
@@ -176,6 +180,342 @@
     return (mixed, attended)
 
 
+MESH = pl.DeviceIdType.MESH
+LANES = 128
+SUBLANES = 8
+
+
+def split_bf16(matrix):
+    high = matrix.astype(jnp.bfloat16)
+    low = (matrix - high.astype(np.float64)).astype(jnp.bfloat16)
+    return high, low
+
+
+def block_transforms(rows):
+    lags = np.arange(-rows, rows, dtype=np.int64)
+    turns = (2 * np.arange(rows, dtype=np.int64)[:, None] + 1) * lags[None, :] % (4 * rows)
+    angles = 2.0 * np.pi / (4 * rows) * turns
+    forward = np.concatenate([np.cos(angles), -np.sin(angles)], axis=0)
+    inverse = forward[:, rows:].T / rows
+    return split_bf16(forward) + split_bf16(inverse)
+
+
+def dot32(left, right):
+    return jnp.dot(left, right, preferred_element_type=jnp.float32)
+
+
+def fused_kernel(
+    shards, fwd_hi, fwd_lo, inv_hi, inv_lo, skip, gate, value, taps, queries, keys,
+    mixed_out, att_out,
+    taps_wide, taps_sent, v_buf, t_buf, g_buf, k_buf, q_buf, v_spec, h_spec, z_spec, m_buf, a_buf,
+    own_sem, in_send, in_recv, out_send, out_recv, own_out,
+):
+    me = lax.axis_index("ctx")
+    rows = value.shape[0]
+    width = v_buf.shape[1]
+    heads = width // HEAD_DIM
+
+    def partner(step):
+        return lax.rem(me + step, shards)
+
+    def block(index):
+        return pl.ds(pl.multiple_of(index * rows, rows), rows)
+
+    def columns(index, size=width, offset=0):
+        return pl.ds(pl.multiple_of(index * width + offset, LANES), size)
+
+    barrier = pltpu.get_barrier_semaphore()
+
+    def greet(step, carry):
+        pl.semaphore_signal(barrier, inc=1, device_id={"ctx": partner(step)}, device_id_type=MESH)
+        return carry
+
+    lax.fori_loop(1, shards, greet, 0)
+
+    wide_copy = pltpu.make_async_copy(taps, taps_wide, own_out.at[0, 0])
+    wide_copy.start()
+
+    streams = [(value, v_buf, width, 0), (taps_sent, t_buf, width, 0), (gate, g_buf, width, 0)]
+    for head in range(heads):
+        streams.append((keys, k_buf.at[head], HEAD_DIM, head * HEAD_DIM))
+        streams.append((queries, q_buf.at[head], HEAD_DIM, head * HEAD_DIM))
+
+    def own_copy(stream):
+        source, target, size, offset = streams[stream]
+        return pltpu.make_async_copy(
+            source.at[:, columns(me, size, offset)], target.at[block(me), :], own_sem.at[stream]
+        )
+
+    def send(stream, step):
+        source, target, size, offset = streams[stream]
+        peer = partner(step)
+        return pltpu.make_async_remote_copy(
+            src_ref=source.at[:, columns(peer, size, offset)],
+            dst_ref=target.at[block(me), :],
+            send_sem=in_send.at[stream, step],
+            recv_sem=in_recv.at[stream, me],
+            device_id={"ctx": peer},
+            device_id_type=MESH,
+        )
+
+    def start_stream(stream):
+        def one(step, carry):
+            send(stream, step).start()
+            return carry
+
+        own_copy(stream).start()
+        lax.fori_loop(1, shards, one, 0)
+
+    def arrived(stream, step):
+        target = streams[stream][1].at[block(partner(step)), :]
+        pltpu.make_async_remote_copy(
+            src_ref=target,
+            dst_ref=target,
+            send_sem=in_send.at[stream, step],
+            recv_sem=in_recv.at[stream, partner(step)],
+            device_id={"ctx": partner(step)},
+            device_id_type=MESH,
+        ).wait_recv()
+
+    def wait_stream(stream):
+        def one(step, carry):
+            arrived(stream, step)
+            return carry
+
+        own_copy(stream).wait()
+        lax.fori_loop(1, shards, one, 0)
+
+    pl.semaphore_wait(barrier, shards - 1)
+    start_stream(0)
+    wide_copy.wait()
+    taps_sent[...] = taps_wide[...].astype(jnp.bfloat16)
+    for stream in range(1, len(streams)):
+        start_stream(stream)
+
+    def spectrum(index):
+        signal = v_buf[block(index), :]
+        v_spec[index] = dot32(fwd_hi[:, rows:], signal) + dot32(fwd_lo[:, rows:], signal)
+
+    own_copy(0).wait()
+    spectrum(me)
+
+    def signal_step(step, carry):
+        arrived(0, step)
+        spectrum(partner(step))
+        return carry
+
+    lax.fori_loop(1, shards, signal_step, 0)
+
+    wait_stream(1)
+    first = t_buf[0:rows, :]
+    h_spec[0] = dot32(fwd_hi[:, rows:], first) + dot32(fwd_lo[:, rows:], first)
+
+    def taps_step(index, carry):
+        window = t_buf[pl.ds(pl.multiple_of((index - 1) * rows, rows), 2 * rows), :]
+        h_spec[index] = dot32(fwd_hi[...], window) + dot32(fwd_lo[...], window)
+        return carry
+
+    lax.fori_loop(1, shards, taps_step, 0)
+
+    def product_step(chunk, carry):
+        real = pl.ds(pl.multiple_of(chunk * SUBLANES, SUBLANES), SUBLANES)
+        imag = pl.ds(pl.multiple_of(rows + chunk * SUBLANES, SUBLANES), SUBLANES)
+        for lane in range(0, width, LANES):
+            part = slice(lane, lane + LANES)
+            v_real = [v_spec[i, real, part] for i in range(shards)]
+            v_imag = [v_spec[i, imag, part] for i in range(shards)]
+            h_real = [h_spec[i, real, part] for i in range(shards)]
+            h_imag = [h_spec[i, imag, part] for i in range(shards)]
+            for out in range(shards):
+                total_real = v_real[0] * h_real[out] - v_imag[0] * h_imag[out]
+                total_imag = v_real[0] * h_imag[out] + v_imag[0] * h_real[out]
+                for i in range(1, out + 1):
+                    total_real += v_real[i] * h_real[out - i] - v_imag[i] * h_imag[out - i]
+                    total_imag += v_real[i] * h_imag[out - i] + v_imag[i] * h_real[out - i]
+                z_spec[out, real, part] = total_real
+                z_spec[out, imag, part] = total_imag
+        return carry
+
+    lax.fori_loop(0, rows // SUBLANES, product_step, 0)
+
+    wait_stream(2)
+    gain = skip[:, columns(me)]
+
+    def mix(index):
+        summed = z_spec[index]
+        high = summed.astype(jnp.bfloat16)
+        low = (summed - high.astype(jnp.float32)).astype(jnp.bfloat16)
+        convolved = dot32(inv_hi[...], high) + dot32(inv_lo[...], high) + dot32(inv_hi[...], low)
+        signal = v_buf[block(index), :].astype(jnp.float32)
+        opened = g_buf[block(index), :].astype(jnp.float32)
+        m_buf[block(index), :] = (opened * (convolved + gain * signal)).astype(jnp.bfloat16)
+
+    def mixed_send(step):
+        peer = partner(step)
+        return pltpu.make_async_remote_copy(
+            src_ref=m_buf.at[block(peer), :],
+            dst_ref=mixed_out.at[:, columns(me)],
+            send_sem=out_send.at[0, step],
+            recv_sem=out_recv.at[0, me],
+            device_id={"ctx": peer},
+            device_id_type=MESH,
+        )
+
+    def mixed_own():
+        return pltpu.make_async_copy(m_buf.at[block(me), :], mixed_out.at[:, columns(me)], own_out.at[0, 0])
+
+    def mix_step(step, carry):
+        mix(partner(step))
+        mixed_send(step).start()
+        return carry
+
+    lax.fori_loop(1, shards, mix_step, 0)
+    mix(me)
+    mixed_own().start()
+
+    scale = math.log2(math.e) / math.sqrt(HEAD_DIM)
+
+    def att_columns(index, head):
+        return pl.ds(pl.multiple_of(index * width + head * HEAD_DIM, LANES), HEAD_DIM)
+
+    def att_send(head, step):
+        peer = partner(step)
+        return pltpu.make_async_remote_copy(
+            src_ref=a_buf.at[head, block(peer), :],
+            dst_ref=att_out.at[:, att_columns(me, head)],
+            send_sem=out_send.at[1 + head, step],
+            recv_sem=out_recv.at[1 + head, me],
+            device_id={"ctx": peer},
+            device_id_type=MESH,
+        )
+
+    def att_own(head):
+        return pltpu.make_async_copy(
+            a_buf.at[head, block(me), :], att_out.at[:, att_columns(me, head)], own_out.at[1, head]
+        )
+
+    def attend(head, index):
+        reach = (index + 1) * rows
+        scores = lax.dot_general(
+            q_buf[head, index * rows : reach, :],
+            k_buf[head, 0:reach, :],
+            (((1,), (1,)), ((), ())),
+            preferred_element_type=jnp.float32,
+        )
+        row = lax.broadcasted_iota(jnp.int32, (rows, rows), 0)
+        column = lax.broadcasted_iota(jnp.int32, (rows, rows), 1)
+        last = jnp.where(column <= row, scores[:, index * rows :], -1e30)
+        if index:
+            scores = jnp.concatenate([scores[:, : index * rows], last], axis=1)
+        else:
+            scores = last
+        highest = jnp.max(scores, axis=1, keepdims=True)
+        weights = jnp.exp2((scores - highest) * scale)
+        total = jnp.sum(weights, axis=1, keepdims=True)
+        part = slice(head * HEAD_DIM, (head + 1) * HEAD_DIM)
+        update = dot32(weights.astype(jnp.bfloat16), m_buf[0:reach, part])
+        a_buf[head, index * rows : reach, :] = (update / total).astype(jnp.bfloat16)
+
+    for head in range(heads):
+        wait_stream(3 + 2 * head)
+        wait_stream(4 + 2 * head)
+
+        def att_step(step, carry, head=head):
+            for index in range(shards):
+                @pl.when(partner(step) == index)
+                def _():
+                    attend(head, index)
+
+            @pl.when(step < shards)
+            def _():
+                att_send(head, step).start()
+
+            return carry
+
+        lax.fori_loop(1, shards + 1, att_step, 0)
+        att_own(head).start()
+
+    mixed_own().wait()
+    for head in range(heads):
+        att_own(head).wait()
+
+    def out_arrived(slot, target, step):
+        pltpu.make_async_remote_copy(
+            src_ref=target,
+            dst_ref=target,
+            send_sem=out_send.at[slot, step],
+            recv_sem=out_recv.at[slot, partner(step)],
+            device_id={"ctx": partner(step)},
+            device_id_type=MESH,
+        ).wait_recv()
+
+    def finish(step, carry):
+        for stream in range(len(streams)):
+            send(stream, step).wait_send()
+        mixed_send(step).wait_send()
+        out_arrived(0, mixed_out.at[:, columns(partner(step))], step)
+        for head in range(heads):
+            att_send(head, step).wait_send()
+            out_arrived(1 + head, att_out.at[:, att_columns(partner(step), head)], step)
+        return carry
+
+    lax.fori_loop(1, shards, finish, 0)
+
+
+def by_heads(gate_input, value_input, filter_taps, skip_gain, queries, keys):
+    shards = lax.axis_size("ctx")
+    rows, channels = value_input.shape
+    width = channels // shards
+    heads = width // HEAD_DIM
+    length = shards * rows
+    streams = 3 + 2 * heads
+    in_place = pl.BlockSpec(memory_space=pl.ANY)
+    in_vmem = pl.BlockSpec(memory_space=pltpu.VMEM)
+    shape = jax.ShapeDtypeStruct((rows, channels), jnp.bfloat16)
+    forward_hi, forward_lo, inverse_hi, inverse_lo = block_transforms(rows)
+    return pl.pallas_call(
+        functools.partial(fused_kernel, shards),
+        out_shape=(shape, shape),
+        in_specs=[in_vmem] * 5 + [in_place] * 5,
+        out_specs=(in_place, in_place),
+        scratch_shapes=[
+            pltpu.VMEM((rows, channels), jnp.float32),
+            pltpu.VMEM((rows, channels), jnp.bfloat16),
+            pltpu.VMEM((length, width), jnp.bfloat16),
+            pltpu.VMEM((length, width), jnp.bfloat16),
+            pltpu.VMEM((length, width), jnp.bfloat16),
+            pltpu.VMEM((heads, length, HEAD_DIM), jnp.bfloat16),
+            pltpu.VMEM((heads, length, HEAD_DIM), jnp.bfloat16),
+            pltpu.VMEM((shards, 2 * rows, width), jnp.float32),
+            pltpu.VMEM((shards, 2 * rows, width), jnp.float32),
+            pltpu.VMEM((shards, 2 * rows, width), jnp.float32),
+            pltpu.VMEM((length, width), jnp.bfloat16),
+            pltpu.VMEM((heads, length, HEAD_DIM), jnp.bfloat16),
+            pltpu.SemaphoreType.DMA((streams,)),
+            pltpu.SemaphoreType.DMA((streams, shards)),
+            pltpu.SemaphoreType.DMA((streams, shards)),
+            pltpu.SemaphoreType.DMA((1 + heads, shards)),
+            pltpu.SemaphoreType.DMA((1 + heads, shards)),
+            pltpu.SemaphoreType.DMA((2, max(heads, 1))),
+        ],
+        compiler_params=pltpu.CompilerParams(
+            collective_id=0, has_side_effects=True, vmem_limit_bytes=56 * 1024 * 1024
+        ),
+        name="conv_attention",
+    )(
+        forward_hi, forward_lo, inverse_hi, inverse_lo, skip_gain.reshape(1, channels),
+        gate_input, value_input, filter_taps, queries, keys,
+    )
+
+
+def per_device(gate_input, value_input, filter_taps, skip_gain, queries, keys):
+    shards = lax.axis_size("ctx")
+    channels = value_input.shape[1]
+    whole_heads = channels % (shards * HEAD_DIM) == 0
+    run = by_heads if whole_heads else by_sequence
+    return run(gate_input, value_input, filter_taps, skip_gain, queries, keys)
+
+
 def solution(mesh):
     placed = (
         P("ctx", "tp"),

time: 469 us -> 91.5 us (0.20); the launches traced: 460 us -> 90.9 us
  waiting for transfers between devices: 124 us -> 0 us
  matrix products: 106 us -> 0 us
  Pallas kernels: 0 us -> 86.9 us
  local copies, waits for them, and re-layouts: 85 us -> 3.37 us
  blocking collectives: 70.7 us -> 0 us
  other arithmetic: 40.6 us -> 0 us
  starting transfers between devices: 19.5 us -> 0 us
  between operations: 14.9 us -> 0.65 us
    dot_general x20 -> x0, matrix products: 106 us -> none  [the longest x12 52.2 us: contract(): return jnp.einsum('qn,knc->kqc', matrix, operand, precision=PRECISE)]
    all_to_all x4 -> x0, waiting for transfers between devices: 104 us -> none  [the longest x1 55.7 us: per_device(): lax.all_to_all(as_sent(spread_front(moved_signal)), 'ctx', split_axis=1,...]
    pallas_call x0 -> x1, Pallas kernels: none -> 86.9 us  [by_heads(): pl.pallas_call(functools.partial(fused_kernel, shards), out_shape=(shape,...]
    all_to_all x2 -> x0, blocking collectives: 70.7 us -> none  [the longest x1 52.7 us: per_device(): lax.all_to_all(as_sent(jnp.stack([real_part, imag_part])), 'ctx', split_a...]
    another operation x3 -> x0, local copies, waits for them, and re-layouts: 19.8 us -> none  [the longest x1 11.2 us: per_device(): jnp.stack([real_part, imag_part])]
    all_gather x2 -> x0, waiting for transfers between devices: 19.7 us -> none  [the longest x1 19.7 us: per_device(): value_block = lax.all_gather(mixed, 'ctx', axis=0, tiled=True)]
    all_to_all x4 -> x0, starting transfers between devices: 19.2 us -> none  [the longest x1 5.44 us: per_device(): lax.all_to_all(filter_taps.reshape(1, tok_rows, channels).astype(jnp.bflo...]
    unnamed x25 -> x4, local copies, waits for them, and re-layouts: 20.3 us -> 3.37 us
  transfers between devices with their start and end apart: 6 -> 0, of which waited for: 5 -> 0; matrix products, arithmetic and copies ran while one was open for 36% -> 0% of each run, Pallas kernels for 0% -> 0%
where the time goes in v1:
time: 91.5 us; the launch traced here: 90.9 us
  Pallas kernels  86.9 us (95%)
  local copies, waits for them, and re-layouts  3.37 us (4%)
    pallas_call x1, Pallas kernels, by_heads(): pl.pallas_call(functools.partial(fused_kernel, shards), out_shape=(shape,...  86.9 us
    unnamed x4, local copies, waits for them, and re-layouts  3.37 us

profile of v1, /device:TPU:0, one launch (start us, length us, event | category | flops | bytes accessed | tf_op | source)
XLA Modules:
  0.0 90.9 jit_solution(758867300349737088)
XLA Ops:
  0.6 86.9 %conv_attention.1 = (bf16[256,2048]{1,0:T(8,128)(2,1)}, bf16[256,2048]{1,0:T(8,128)(2,1)}) custom-call(bf16[512,512]{1,0:T(8,128)(2,1)} %constant.8.clone.fwd_hi, bf16[512,512]{1,0:T(8,128)(2,1)} %constant.9.clone.fwd_lo, bf16[256,512]{1,0:T(8,128)(2,1)} %constant.10.clone.inv_hi, bf16[256,512]{1,0:T(8,128)(2,1)} %constant.11.clone.inv_lo, ...), custom_call_target="tpu_custom_call" | custom-call | tf_op jit(solution)/shard_map/conv_attention/pallas_call | solution.py:476
  87.6 0.0 copy-start
  87.6 2.4 %copy.14 = bf16[256,2048]{1,0:T(8,128)(2,1)} copy(bf16[256,2048]{1,0:T(8,128)(2,1)} %get-tuple-element.4) | data formatting | bytes 2097152
  90.0 0.0 copy-done
  90.0 1.0 %copy.15 = bf16[256,2048]{1,0:T(8,128)(2,1)} copy(bf16[256,2048]{1,0:T(8,128)(2,1)S(1)} %copy-done) | data formatting | bytes 2097152
Async XLA Ops:
  87.6 2.4 %copy-start = (bf16[256,2048]{1,0:T(8,128)(2,1)S(1)}, bf16[256,2048]{1,0:T(8,128)(2,1)}, u32[]{:S(2)}) copy-start(bf16[256,2048]{1,0:T(8,128)(2,1)} %get-tuple-element.5) | copy-start | bytes 3145732

commit v2 on v1

--- a/solution.py
+++ b/solution.py
@@ -216,7 +216,20 @@
     heads = width // HEAD_DIM
 
     def partner(step):
-        return lax.rem(me + step, shards)
+        if shards % 4:
+            return lax.rem(me + step, shards)
+        outer = shards // 4
+        core = me % 2
+        turn = step // 2
+        along_x = (1 - core) * (turn % 2) + core * (turn // outer)
+        along_y = (1 - core) * (turn // 2) + core * (turn % outer)
+        new_core = (core + step) % 2
+        new_x = (me // 2 + along_x) % 2
+        new_y = (me // 4 + along_y) % outer
+        return (new_y * 2 + new_x) * 2 + new_core
+
+    def ordered(turn):
+        return turn % (shards - 1) + 1 + (turn // shards) * (shards - 2)
 
     def block(index):
         return pl.ds(pl.multiple_of(index * rows, rows), rows)
@@ -259,8 +272,8 @@
         )
 
     def start_stream(stream):
-        def one(step, carry):
-            send(stream, step).start()
+        def one(turn, carry):
+            send(stream, ordered(turn)).start()
             return carry
 
         own_copy(stream).start()
@@ -289,8 +302,7 @@
     start_stream(0)
     wide_copy.wait()
     taps_sent[...] = taps_wide[...].astype(jnp.bfloat16)
-    for stream in range(1, len(streams)):
-        start_stream(stream)
+    start_stream(1)
 
     def spectrum(index):
         signal = v_buf[block(index), :]
@@ -299,14 +311,18 @@
     own_copy(0).wait()
     spectrum(me)
 
-    def signal_step(step, carry):
+    def signal_step(turn, carry):
+        step = ordered(turn)
         arrived(0, step)
         spectrum(partner(step))
         return carry
 
     lax.fori_loop(1, shards, signal_step, 0)
 
+    start_stream(2)
     wait_stream(1)
+    for stream in range(3, min(5, len(streams))):
+        start_stream(stream)
     first = t_buf[0:rows, :]
     h_spec[0] = dot32(fwd_hi[:, rows:], first) + dot32(fwd_lo[:, rows:], first)
 
@@ -339,6 +355,8 @@
     lax.fori_loop(0, rows // SUBLANES, product_step, 0)
 
     wait_stream(2)
+    for stream in range(5, len(streams)):
+        start_stream(stream)
     gain = skip[:, columns(me)]
 
     def mix(index):
@@ -364,7 +382,8 @@
     def mixed_own():
         return pltpu.make_async_copy(m_buf.at[block(me), :], mixed_out.at[:, columns(me)], own_out.at[0, 0])
 
-    def mix_step(step, carry):
+    def mix_step(turn, carry):
+        step = ordered(turn)
         mix(partner(step))
         mixed_send(step).start()
         return carry
@@ -420,13 +439,14 @@
         wait_stream(3 + 2 * head)
         wait_stream(4 + 2 * head)
 
-        def att_step(step, carry, head=head):
+        def att_step(turn, carry, head=head):
+            step = ordered(turn)
             for index in range(shards):
                 @pl.when(partner(step) == index)
                 def _():
                     attend(head, index)
 
-            @pl.when(step < shards)
+            @pl.when(turn < shards)
             def _():
                 att_send(head, step).start()
 

time: 91.5 us -> 91.4 us (level)
  no operation moved by 1% of the time
where the time goes in v2:
time: 91.4 us; the launch traced here: 91.2 us
  Pallas kernels  87.2 us (95%)
  local copies, waits for them, and re-layouts  3.37 us (4%)
    pallas_call x1, Pallas kernels, by_heads(): pl.pallas_call(functools.partial(fused_kernel, shards), out_shape=(shape,...  87.2 us
    unnamed x4, local copies, waits for them, and re-layouts  3.37 us

profile of v2, /device:TPU:0, one launch (start us, length us, event | category | flops | bytes accessed | tf_op | source)
XLA Modules:
  0.0 91.2 jit_solution(817418367235431306)
XLA Ops:
  0.6 87.2 %conv_attention.1 = (bf16[256,2048]{1,0:T(8,128)(2,1)}, bf16[256,2048]{1,0:T(8,128)(2,1)}) custom-call(bf16[512,512]{1,0:T(8,128)(2,1)} %constant.8.clone.fwd_hi, bf16[512,512]{1,0:T(8,128)(2,1)} %constant.9.clone.fwd_lo, bf16[256,512]{1,0:T(8,128)(2,1)} %constant.10.clone.inv_hi, bf16[256,512]{1,0:T(8,128)(2,1)} %constant.11.clone.inv_lo, ...), custom_call_target="tpu_custom_call" | custom-call | tf_op jit(solution)/shard_map/conv_attention/pallas_call | solution.py:496
  87.8 0.0 copy-start
  87.9 2.4 %copy.14 = bf16[256,2048]{1,0:T(8,128)(2,1)} copy(bf16[256,2048]{1,0:T(8,128)(2,1)} %get-tuple-element.4) | data formatting | bytes 2097152
  90.2 0.0 copy-done
  90.3 1.0 %copy.15 = bf16[256,2048]{1,0:T(8,128)(2,1)} copy(bf16[256,2048]{1,0:T(8,128)(2,1)S(1)} %copy-done) | data formatting | bytes 2097152
Async XLA Ops:
  87.8 2.4 %copy-start = (bf16[256,2048]{1,0:T(8,128)(2,1)S(1)}, bf16[256,2048]{1,0:T(8,128)(2,1)}, u32[]{:S(2)}) copy-start(bf16[256,2048]{1,0:T(8,128)(2,1)} %get-tuple-element.5) | copy-start | bytes 3145732

commit v3 on v2

--- a/solution.py
+++ b/solution.py
@@ -208,6 +208,7 @@
     shards, fwd_hi, fwd_lo, inv_hi, inv_lo, skip, gate, value, taps, queries, keys,
     mixed_out, att_out,
     taps_wide, taps_sent, v_buf, t_buf, g_buf, k_buf, q_buf, v_spec, h_spec, z_spec, m_buf, a_buf,
+    s_buf, p_buf, l_buf,
     own_sem, in_send, in_recv, out_send, out_recv, own_out,
 ):
     me = lax.axis_index("ctx")
@@ -415,25 +416,39 @@
 
     def attend(head, index):
         reach = (index + 1) * rows
-        scores = lax.dot_general(
-            q_buf[head, index * rows : reach, :],
+        before = index * rows
+        s_buf[:, 0:reach] = lax.dot_general(
+            q_buf[head, before:reach, :],
             k_buf[head, 0:reach, :],
             (((1,), (1,)), ((), ())),
             preferred_element_type=jnp.float32,
         )
-        row = lax.broadcasted_iota(jnp.int32, (rows, rows), 0)
-        column = lax.broadcasted_iota(jnp.int32, (rows, rows), 1)
-        last = jnp.where(column <= row, scores[:, index * rows :], -1e30)
-        if index:
-            scores = jnp.concatenate([scores[:, : index * rows], last], axis=1)
-        else:
-            scores = last
-        highest = jnp.max(scores, axis=1, keepdims=True)
-        weights = jnp.exp2((scores - highest) * scale)
-        total = jnp.sum(weights, axis=1, keepdims=True)
+        tile = 16 if reach > 4 * rows else 32
+
+        def softmax_tile(turn, carry):
+            span = pl.ds(pl.multiple_of(turn * tile, tile), tile)
+            row = lax.broadcasted_iota(jnp.int32, (tile, rows), 0) + turn * tile
+            column = lax.broadcasted_iota(jnp.int32, (tile, rows), 1)
+            last = jnp.where(column <= row, s_buf[span, before:reach], -1e30)
+            highest = jnp.max(last, axis=1, keepdims=True)
+            if index:
+                early = s_buf[span, 0:before]
+                highest = jnp.maximum(highest, jnp.max(early, axis=1, keepdims=True))
+            top = highest * scale
+            last = jnp.exp2(last * scale - top)
+            total = jnp.sum(last, axis=1, keepdims=True)
+            p_buf[span, before:reach] = last.astype(jnp.bfloat16)
+            if index:
+                early = jnp.exp2(early * scale - top)
+                total += jnp.sum(early, axis=1, keepdims=True)
+                p_buf[span, 0:before] = early.astype(jnp.bfloat16)
+            l_buf[span, :] = jnp.broadcast_to(total, (tile, HEAD_DIM))
+            return carry
+
+        lax.fori_loop(0, rows // tile, softmax_tile, 0, unroll=2)
         part = slice(head * HEAD_DIM, (head + 1) * HEAD_DIM)
-        update = dot32(weights.astype(jnp.bfloat16), m_buf[0:reach, part])
-        a_buf[head, index * rows : reach, :] = (update / total).astype(jnp.bfloat16)
+        update = dot32(p_buf[:, 0:reach], m_buf[0:reach, part])
+        a_buf[head, before:reach, :] = (update / l_buf[...]).astype(jnp.bfloat16)
 
     for head in range(heads):
         wait_stream(3 + 2 * head)
@@ -493,7 +508,7 @@
     in_vmem = pl.BlockSpec(memory_space=pltpu.VMEM)
     shape = jax.ShapeDtypeStruct((rows, channels), jnp.bfloat16)
     forward_hi, forward_lo, inverse_hi, inverse_lo = block_transforms(rows)
-    return pl.pallas_call(
+    results = pl.pallas_call(
         functools.partial(fused_kernel, shards),
         out_shape=(shape, shape),
         in_specs=[in_vmem] * 5 + [in_place] * 5,
@@ -511,6 +526,9 @@
             pltpu.VMEM((shards, 2 * rows, width), jnp.float32),
             pltpu.VMEM((length, width), jnp.bfloat16),
             pltpu.VMEM((heads, length, HEAD_DIM), jnp.bfloat16),
+            pltpu.VMEM((rows, length), jnp.float32),
+            pltpu.VMEM((rows, length), jnp.bfloat16),
+            pltpu.VMEM((rows, HEAD_DIM), jnp.float32),
             pltpu.SemaphoreType.DMA((streams,)),
             pltpu.SemaphoreType.DMA((streams, shards)),
             pltpu.SemaphoreType.DMA((streams, shards)),
@@ -526,6 +544,31 @@
         forward_hi, forward_lo, inverse_hi, inverse_lo, skip_gain.reshape(1, channels),
         gate_input, value_input, filter_taps, queries, keys,
     )
+    return pl.pallas_call(
+        hand_over,
+        out_shape=(shape, shape),
+        in_specs=[in_place] * 2,
+        out_specs=(in_place, in_place),
+        scratch_shapes=[pltpu.SemaphoreType.DMA((2, HAND_OVERS))],
+        compiler_params=pltpu.CompilerParams(vmem_limit_bytes=56 * 1024 * 1024),
+        name="hand_over",
+    )(*results)
+
+
+HAND_OVERS = 4
+
+
+def hand_over(first, second, first_out, second_out, sems):
+    rows = first.shape[0] // HAND_OVERS
+    copies = []
+    for number, (source, target) in enumerate(((first, first_out), (second, second_out))):
+        for part in range(HAND_OVERS):
+            span = pl.ds(part * rows, rows)
+            copies.append(pltpu.make_async_copy(source.at[span, :], target.at[span, :], sems.at[number, part]))
+    for copy in copies:
+        copy.start()
+    for copy in copies:
+        copy.wait()
 
 
 def per_device(gate_input, value_input, filter_taps, skip_gain, queries, keys):

time: 91.4 us -> 153 us (1.67)
  Pallas kernels: 87.2 us -> 152 us
  local copies, waits for them, and re-layouts: 3.37 us -> 0 us
    pallas_call x0 -> x1, Pallas kernels: none -> 64.7 us  [by_heads(): pl.pallas_call(hand_over, out_shape=(shape, shape), in_specs=[in_place] *...]
    unnamed x4 -> x0, local copies, waits for them, and re-layouts: 3.37 us -> none
where the time goes in v3:
time: 153 us
  Pallas kernels  152 us (99%)
    pallas_call x1, Pallas kernels, by_heads(): pl.pallas_call(functools.partial(fused_kernel, shards), out_shape=(shape,...  87.2 us
    pallas_call x1, Pallas kernels, by_heads(): pl.pallas_call(hand_over, out_shape=(shape, shape), in_specs=[in_place] *...  64.7 us

profile of v3, /device:TPU:0, one launch (start us, length us, event | category | flops | bytes accessed | tf_op | source)
XLA Modules:
  0.0 152.6 jit_solution(13811573810542797136)
XLA Ops:
  0.6 87.2 %conv_attention.1 = (bf16[256,2048]{1,0:T(8,128)(2,1)}, bf16[256,2048]{1,0:T(8,128)(2,1)}) custom-call(bf16[512,512]{1,0:T(8,128)(2,1)} %constant.8.clone.fwd_hi, bf16[512,512]{1,0:T(8,128)(2,1)} %constant.9.clone.fwd_lo, bf16[256,512]{1,0:T(8,128)(2,1)} %constant.10.clone.inv_hi, bf16[256,512]{1,0:T(8,128)(2,1)} %constant.11.clone.inv_lo, ...), custom_call_target="tpu_custom_call" | custom-call | tf_op jit(solution)/shard_map/conv_attention/pallas_call | solution.py:511
  87.8 64.7 %hand_over.1 = (bf16[256,2048]{1,0:T(8,128)(2,1)}, bf16[256,2048]{1,0:T(8,128)(2,1)}) custom-call(bf16[256,2048]{1,0:T(8,128)(2,1)} %get-tuple-element.4.first, bf16[256,2048]{1,0:T(8,128)(2,1)} %get-tuple-element.5.second), custom_call_target="tpu_custom_call" | custom-call | tf_op jit(solution)/shard_map/hand_over/pallas_call | solution.py:547

commit v4 on v3

--- a/solution.py
+++ b/solution.py
@@ -208,8 +208,8 @@
     shards, fwd_hi, fwd_lo, inv_hi, inv_lo, skip, gate, value, taps, queries, keys,
     mixed_out, att_out,
     taps_wide, taps_sent, v_buf, t_buf, g_buf, k_buf, q_buf, v_spec, h_spec, z_spec, m_buf, a_buf,
-    s_buf, p_buf, l_buf,
-    own_sem, in_send, in_recv, out_send, out_recv, own_out,
+    s_buf, p_buf, l_buf, v_sent, g_sent, k_sent, q_sent, mixed_in, att_in,
+    own_sem, in_send, in_recv, out_send, out_recv, own_out, stage_sem, end_sem,
 ):
     me = lax.axis_index("ctx")
     rows = value.shape[0]
@@ -247,12 +247,21 @@
     lax.fori_loop(1, shards, greet, 0)
 
     wide_copy = pltpu.make_async_copy(taps, taps_wide, own_out.at[0, 0])
+    staged = [
+        pltpu.make_async_copy(source, target, stage_sem.at[number])
+        for number, (source, target) in enumerate(
+            ((value, v_sent), (gate, g_sent), (keys, k_sent), (queries, q_sent))
+        )
+    ]
+    staged[0].start()
     wide_copy.start()
-
-    streams = [(value, v_buf, width, 0), (taps_sent, t_buf, width, 0), (gate, g_buf, width, 0)]
+    for copy in staged[1:]:
+        copy.start()
+
+    streams = [(v_sent, v_buf, width, 0), (taps_sent, t_buf, width, 0), (g_sent, g_buf, width, 0)]
     for head in range(heads):
-        streams.append((keys, k_buf.at[head], HEAD_DIM, head * HEAD_DIM))
-        streams.append((queries, q_buf.at[head], HEAD_DIM, head * HEAD_DIM))
+        streams.append((k_sent, k_buf.at[head], HEAD_DIM, head * HEAD_DIM))
+        streams.append((q_sent, q_buf.at[head], HEAD_DIM, head * HEAD_DIM))
 
     def own_copy(stream):
         source, target, size, offset = streams[stream]
@@ -300,6 +309,7 @@
         lax.fori_loop(1, shards, one, 0)
 
     pl.semaphore_wait(barrier, shards - 1)
+    staged[0].wait()
     start_stream(0)
     wide_copy.wait()
     taps_sent[...] = taps_wide[...].astype(jnp.bfloat16)
@@ -320,8 +330,11 @@
 
     lax.fori_loop(1, shards, signal_step, 0)
 
+    staged[1].wait()
     start_stream(2)
     wait_stream(1)
+    staged[2].wait()
+    staged[3].wait()
     for stream in range(3, min(5, len(streams))):
         start_stream(stream)
     first = t_buf[0:rows, :]
@@ -373,7 +386,7 @@
         peer = partner(step)
         return pltpu.make_async_remote_copy(
             src_ref=m_buf.at[block(peer), :],
-            dst_ref=mixed_out.at[:, columns(me)],
+            dst_ref=mixed_in.at[:, columns(me)],
             send_sem=out_send.at[0, step],
             recv_sem=out_recv.at[0, me],
             device_id={"ctx": peer},
@@ -381,7 +394,7 @@
         )
 
     def mixed_own():
-        return pltpu.make_async_copy(m_buf.at[block(me), :], mixed_out.at[:, columns(me)], own_out.at[0, 0])
+        return pltpu.make_async_copy(m_buf.at[block(me), :], mixed_in.at[:, columns(me)], own_out.at[0, 0])
 
     def mix_step(turn, carry):
         step = ordered(turn)
@@ -402,7 +415,7 @@
         peer = partner(step)
         return pltpu.make_async_remote_copy(
             src_ref=a_buf.at[head, block(peer), :],
-            dst_ref=att_out.at[:, att_columns(me, head)],
+            dst_ref=att_in.at[:, att_columns(me, head)],
             send_sem=out_send.at[1 + head, step],
             recv_sem=out_recv.at[1 + head, me],
             device_id={"ctx": peer},
@@ -411,7 +424,7 @@
 
     def att_own(head):
         return pltpu.make_async_copy(
-            a_buf.at[head, block(me), :], att_out.at[:, att_columns(me, head)], own_out.at[1, head]
+            a_buf.at[head, block(me), :], att_in.at[:, att_columns(me, head)], own_out.at[1, head]
         )
 
     def attend(head, index):
@@ -484,17 +497,28 @@
             device_id_type=MESH,
         ).wait_recv()
 
+    def mixed_finish(step, carry):
+        out_arrived(0, mixed_in.at[:, columns(partner(step))], step)
+        return carry
+
+    lax.fori_loop(1, shards, mixed_finish, 0)
+    mixed_end = pltpu.make_async_copy(mixed_in, mixed_out, end_sem.at[0])
+    mixed_end.start()
+
     def finish(step, carry):
         for stream in range(len(streams)):
             send(stream, step).wait_send()
         mixed_send(step).wait_send()
-        out_arrived(0, mixed_out.at[:, columns(partner(step))], step)
         for head in range(heads):
             att_send(head, step).wait_send()
-            out_arrived(1 + head, att_out.at[:, att_columns(partner(step), head)], step)
+            out_arrived(1 + head, att_in.at[:, att_columns(partner(step), head)], step)
         return carry
 
     lax.fori_loop(1, shards, finish, 0)
+    att_end = pltpu.make_async_copy(att_in, att_out, end_sem.at[1])
+    att_end.start()
+    mixed_end.wait()
+    att_end.wait()
 
 
 def by_heads(gate_input, value_input, filter_taps, skip_gain, queries, keys):
@@ -529,12 +553,17 @@
             pltpu.VMEM((rows, length), jnp.float32),
             pltpu.VMEM((rows, length), jnp.bfloat16),
             pltpu.VMEM((rows, HEAD_DIM), jnp.float32),
+        ]
+        + [pltpu.VMEM((rows, channels), jnp.bfloat16)] * 6
+        + [
             pltpu.SemaphoreType.DMA((streams,)),
             pltpu.SemaphoreType.DMA((streams, shards)),
             pltpu.SemaphoreType.DMA((streams, shards)),
             pltpu.SemaphoreType.DMA((1 + heads, shards)),
             pltpu.SemaphoreType.DMA((1 + heads, shards)),
             pltpu.SemaphoreType.DMA((2, max(heads, 1))),
+            pltpu.SemaphoreType.DMA((4,)),
+            pltpu.SemaphoreType.DMA((2,)),
         ],
         compiler_params=pltpu.CompilerParams(
             collective_id=0, has_side_effects=True, vmem_limit_bytes=56 * 1024 * 1024
@@ -549,7 +578,8 @@
         out_shape=(shape, shape),
         in_specs=[in_place] * 2,
         out_specs=(in_place, in_place),
-        scratch_shapes=[pltpu.SemaphoreType.DMA((2, HAND_OVERS))],
+        scratch_shapes=[pltpu.VMEM((2, rows, channels), jnp.bfloat16)]
+        + [pltpu.SemaphoreType.DMA((2, HAND_OVERS))] * 2,
         compiler_params=pltpu.CompilerParams(vmem_limit_bytes=56 * 1024 * 1024),
         name="hand_over",
     )(*results)
@@ -558,16 +588,21 @@
 HAND_OVERS = 4
 
 
-def hand_over(first, second, first_out, second_out, sems):
+def hand_over(first, second, first_out, second_out, held, in_sems, out_sems):
     rows = first.shape[0] // HAND_OVERS
-    copies = []
-    for number, (source, target) in enumerate(((first, first_out), (second, second_out))):
-        for part in range(HAND_OVERS):
-            span = pl.ds(part * rows, rows)
-            copies.append(pltpu.make_async_copy(source.at[span, :], target.at[span, :], sems.at[number, part]))
-    for copy in copies:
+    arriving, leaving = [], []
+    for part in range(HAND_OVERS):
+        span = pl.ds(part * rows, rows)
+        for number, (source, target) in enumerate(((first, first_out), (second, second_out))):
+            slot = held.at[number, span, :]
+            arriving.append(pltpu.make_async_copy(source.at[span, :], slot, in_sems.at[number, part]))
+            leaving.append(pltpu.make_async_copy(slot, target.at[span, :], out_sems.at[number, part]))
+    for copy in arriving:
         copy.start()
-    for copy in copies:
+    for copy, onward in zip(arriving, leaving):
+        copy.wait()
+        onward.start()
+    for copy in leaving:
         copy.wait()
 
 

time: 153 us -> 91.6 us (0.60)
  Pallas kernels: 152 us -> 90.7 us
    pallas_call x1, Pallas kernels: 64.7 us -> 2.39 us  [by_heads(): pl.pallas_call(hand_over, out_shape=(shape, shape), in_specs=[in_place] *...]
where the time goes in v4:
time: 91.6 us; the launch traced here: 91.3 us
  Pallas kernels  90.7 us (99%)
    pallas_call x1, Pallas kernels, by_heads(): pl.pallas_call(functools.partial(fused_kernel, shards), out_shape=(shape,...  88.3 us
    pallas_call x1, Pallas kernels, by_heads(): pl.pallas_call(hand_over, out_shape=(shape, shape), in_specs=[in_place] *...  2.39 us

profile of v4, /device:TPU:0, one launch (start us, length us, event | category | flops | bytes accessed | tf_op | source)
XLA Modules:
  0.0 91.3 jit_solution(18382826045843425990)
XLA Ops:
  0.6 88.3 %conv_attention.1 = (bf16[256,2048]{1,0:T(8,128)(2,1)}, bf16[256,2048]{1,0:T(8,128)(2,1)}) custom-call(bf16[512,512]{1,0:T(8,128)(2,1)} %constant.8.clone.fwd_hi, bf16[512,512]{1,0:T(8,128)(2,1)} %constant.9.clone.fwd_lo, bf16[256,512]{1,0:T(8,128)(2,1)} %constant.10.clone.inv_hi, bf16[256,512]{1,0:T(8,128)(2,1)} %constant.11.clone.inv_lo, ...), custom_call_target="tpu_custom_call" | custom-call | tf_op jit(solution)/shard_map/conv_attention/pallas_call | solution.py:535
  88.9 2.4 %hand_over.1 = (bf16[256,2048]{1,0:T(8,128)(2,1)}, bf16[256,2048]{1,0:T(8,128)(2,1)}) custom-call(bf16[256,2048]{1,0:T(8,128)(2,1)} %get-tuple-element.4.first, bf16[256,2048]{1,0:T(8,128)(2,1)} %get-tuple-element.5.second), custom_call_target="tpu_custom_call" | custom-call | tf_op jit(solution)/shard_map/hand_over/pallas_call | solution.py:576

commit v5 on v3

--- a/solution.py
+++ b/solution.py
@@ -205,11 +205,11 @@
 
 
 def fused_kernel(
-    shards, fwd_hi, fwd_lo, inv_hi, inv_lo, skip, gate, value, taps, queries, keys,
-    mixed_out, att_out,
+    shards, fwd_hi_in, fwd_lo_in, inv_hi_in, inv_lo_in, skip_in, gate, value, taps, queries, keys,
+    mixed_in, att_in,
     taps_wide, taps_sent, v_buf, t_buf, g_buf, k_buf, q_buf, v_spec, h_spec, z_spec, m_buf, a_buf,
-    s_buf, p_buf, l_buf,
-    own_sem, in_send, in_recv, out_send, out_recv, own_out,
+    s_buf, p_buf, l_buf, fwd_hi, fwd_lo, inv_hi, inv_lo, skip,
+    own_sem, in_send, in_recv, out_send, out_recv, own_out, stage_sem,
 ):
     me = lax.axis_index("ctx")
     rows = value.shape[0]
@@ -235,8 +235,8 @@
     def block(index):
         return pl.ds(pl.multiple_of(index * rows, rows), rows)
 
-    def columns(index, size=width, offset=0):
-        return pl.ds(pl.multiple_of(index * width + offset, LANES), size)
+    def columns(index):
+        return pl.ds(pl.multiple_of(index * width, LANES), width)
 
     barrier = pltpu.get_barrier_semaphore()
 
@@ -246,25 +246,30 @@
 
     lax.fori_loop(1, shards, greet, 0)
 
-    wide_copy = pltpu.make_async_copy(taps, taps_wide, own_out.at[0, 0])
+    wide_copy = pltpu.make_async_copy(taps, taps_wide, own_out.at[0])
     wide_copy.start()
-
-    streams = [(value, v_buf, width, 0), (taps_sent, t_buf, width, 0), (gate, g_buf, width, 0)]
-    for head in range(heads):
-        streams.append((keys, k_buf.at[head], HEAD_DIM, head * HEAD_DIM))
-        streams.append((queries, q_buf.at[head], HEAD_DIM, head * HEAD_DIM))
+    staged = [
+        pltpu.make_async_copy(source, target, stage_sem.at[number])
+        for number, (source, target) in enumerate(
+            (
+                (fwd_hi_in, fwd_hi), (fwd_lo_in, fwd_lo), (skip_in, skip),
+                (inv_hi_in, inv_hi), (inv_lo_in, inv_lo),
+            )
+        )
+    ]
+    streams = [(value, v_buf), (taps_sent, t_buf), (gate, g_buf), (keys, k_buf), (queries, q_buf)]
 
     def own_copy(stream):
-        source, target, size, offset = streams[stream]
+        source, target = streams[stream]
         return pltpu.make_async_copy(
-            source.at[:, columns(me, size, offset)], target.at[block(me), :], own_sem.at[stream]
+            source.at[:, columns(me)], target.at[block(me), :], own_sem.at[stream]
         )
 
     def send(stream, step):
-        source, target, size, offset = streams[stream]
+        source, target = streams[stream]
         peer = partner(step)
         return pltpu.make_async_remote_copy(
-            src_ref=source.at[:, columns(peer, size, offset)],
+            src_ref=source.at[:, columns(peer)],
             dst_ref=target.at[block(me), :],
             send_sem=in_send.at[stream, step],
             recv_sem=in_recv.at[stream, me],
@@ -301,6 +306,8 @@
 
     pl.semaphore_wait(barrier, shards - 1)
     start_stream(0)
+    for copy in staged:
+        copy.start()
     wide_copy.wait()
     taps_sent[...] = taps_wide[...].astype(jnp.bfloat16)
     start_stream(1)
@@ -309,6 +316,8 @@
         signal = v_buf[block(index), :]
         v_spec[index] = dot32(fwd_hi[:, rows:], signal) + dot32(fwd_lo[:, rows:], signal)
 
+    for copy in staged:
+        copy.wait()
     own_copy(0).wait()
     spectrum(me)
 
@@ -322,8 +331,8 @@
 
     start_stream(2)
     wait_stream(1)
-    for stream in range(3, min(5, len(streams))):
-        start_stream(stream)
+    start_stream(3)
+    start_stream(4)
     first = t_buf[0:rows, :]
     h_spec[0] = dot32(fwd_hi[:, rows:], first) + dot32(fwd_lo[:, rows:], first)
 
@@ -356,8 +365,6 @@
     lax.fori_loop(0, rows // SUBLANES, product_step, 0)
 
     wait_stream(2)
-    for stream in range(5, len(streams)):
-        start_stream(stream)
     gain = skip[:, columns(me)]
 
     def mix(index):
@@ -373,7 +380,7 @@
         peer = partner(step)
         return pltpu.make_async_remote_copy(
             src_ref=m_buf.at[block(peer), :],
-            dst_ref=mixed_out.at[:, columns(me)],
+            dst_ref=mixed_in.at[:, columns(me)],
             send_sem=out_send.at[0, step],
             recv_sem=out_recv.at[0, me],
             device_id={"ctx": peer},
@@ -381,7 +388,7 @@
         )
 
     def mixed_own():
-        return pltpu.make_async_copy(m_buf.at[block(me), :], mixed_out.at[:, columns(me)], own_out.at[0, 0])
+        return pltpu.make_async_copy(m_buf.at[block(me), :], mixed_in.at[:, columns(me)], own_out.at[0])
 
     def mix_step(turn, carry):
         step = ordered(turn)
@@ -395,31 +402,27 @@
 
     scale = math.log2(math.e) / math.sqrt(HEAD_DIM)
 
-    def att_columns(index, head):
-        return pl.ds(pl.multiple_of(index * width + head * HEAD_DIM, LANES), HEAD_DIM)
-
-    def att_send(head, step):
+    def att_send(step):
         peer = partner(step)
         return pltpu.make_async_remote_copy(
-            src_ref=a_buf.at[head, block(peer), :],
-            dst_ref=att_out.at[:, att_columns(me, head)],
-            send_sem=out_send.at[1 + head, step],
-            recv_sem=out_recv.at[1 + head, me],
+            src_ref=a_buf.at[block(peer), :],
+            dst_ref=att_in.at[:, columns(me)],
+            send_sem=out_send.at[1, step],
+            recv_sem=out_recv.at[1, me],
             device_id={"ctx": peer},
             device_id_type=MESH,
         )
 
-    def att_own(head):
-        return pltpu.make_async_copy(
-            a_buf.at[head, block(me), :], att_out.at[:, att_columns(me, head)], own_out.at[1, head]
-        )
+    def att_own():
+        return pltpu.make_async_copy(a_buf.at[block(me), :], att_in.at[:, columns(me)], own_out.at[1])
 
     def attend(head, index):
         reach = (index + 1) * rows
         before = index * rows
+        part = slice(head * HEAD_DIM, (head + 1) * HEAD_DIM)
         s_buf[:, 0:reach] = lax.dot_general(
-            q_buf[head, before:reach, :],
-            k_buf[head, 0:reach, :],
+            q_buf[before:reach, part],
+            k_buf[0:reach, part],
             (((1,), (1,)), ((), ())),
             preferred_element_type=jnp.float32,
         )
@@ -446,33 +449,30 @@
             return carry
 
         lax.fori_loop(0, rows // tile, softmax_tile, 0, unroll=2)
-        part = slice(head * HEAD_DIM, (head + 1) * HEAD_DIM)
         update = dot32(p_buf[:, 0:reach], m_buf[0:reach, part])
-        a_buf[head, before:reach, :] = (update / l_buf[...]).astype(jnp.bfloat16)
-
-    for head in range(heads):
-        wait_stream(3 + 2 * head)
-        wait_stream(4 + 2 * head)
-
-        def att_step(turn, carry, head=head):
-            step = ordered(turn)
-            for index in range(shards):
-                @pl.when(partner(step) == index)
-                def _():
+        a_buf[before:reach, part] = (update / l_buf[...]).astype(jnp.bfloat16)
+
+    wait_stream(3)
+    wait_stream(4)
+
+    def att_step(turn, carry):
+        step = ordered(turn)
+        for index in range(shards):
+            @pl.when(partner(step) == index)
+            def _():
+                for head in range(heads):
                     attend(head, index)
 
-            @pl.when(turn < shards)
-            def _():
-                att_send(head, step).start()
-
-            return carry
-
-        lax.fori_loop(1, shards + 1, att_step, 0)
-        att_own(head).start()
-
+        @pl.when(turn < shards)
+        def _():
+            att_send(step).start()
+
+        return carry
+
+    lax.fori_loop(1, shards + 1, att_step, 0)
+    att_own().start()
     mixed_own().wait()
-    for head in range(heads):
-        att_own(head).wait()
+    att_own().wait()
 
     def out_arrived(slot, target, step):
         pltpu.make_async_remote_copy(
@@ -488,10 +488,9 @@
         for stream in range(len(streams)):
             send(stream, step).wait_send()
         mixed_send(step).wait_send()
-        out_arrived(0, mixed_out.at[:, columns(partner(step))], step)
-        for head in range(heads):
-            att_send(head, step).wait_send()
-            out_arrived(1 + head, att_out.at[:, att_columns(partner(step), head)], step)
+        att_send(step).wait_send()
+        out_arrived(0, mixed_in.at[:, columns(partner(step))], step)
+        out_arrived(1, att_in.at[:, columns(partner(step))], step)
         return carry
 
     lax.fori_loop(1, shards, finish, 0)
@@ -501,17 +500,16 @@
     shards = lax.axis_size("ctx")
     rows, channels = value_input.shape
     width = channels // shards
-    heads = width // HEAD_DIM
     length = shards * rows
-    streams = 3 + 2 * heads
+    streams = 5
     in_place = pl.BlockSpec(memory_space=pl.ANY)
-    in_vmem = pl.BlockSpec(memory_space=pltpu.VMEM)
+    landing = pltpu.VMEM((rows, channels), jnp.bfloat16)
     shape = jax.ShapeDtypeStruct((rows, channels), jnp.bfloat16)
     forward_hi, forward_lo, inverse_hi, inverse_lo = block_transforms(rows)
     results = pl.pallas_call(
         functools.partial(fused_kernel, shards),
-        out_shape=(shape, shape),
-        in_specs=[in_vmem] * 5 + [in_place] * 5,
+        out_shape=(landing, landing),
+        in_specs=[in_place] * 10,
         out_specs=(in_place, in_place),
         scratch_shapes=[
             pltpu.VMEM((rows, channels), jnp.float32),
@@ -519,22 +517,28 @@
             pltpu.VMEM((length, width), jnp.bfloat16),
             pltpu.VMEM((length, width), jnp.bfloat16),
             pltpu.VMEM((length, width), jnp.bfloat16),
-            pltpu.VMEM((heads, length, HEAD_DIM), jnp.bfloat16),
-            pltpu.VMEM((heads, length, HEAD_DIM), jnp.bfloat16),
+            pltpu.VMEM((length, width), jnp.bfloat16),
+            pltpu.VMEM((length, width), jnp.bfloat16),
             pltpu.VMEM((shards, 2 * rows, width), jnp.float32),
             pltpu.VMEM((shards, 2 * rows, width), jnp.float32),
             pltpu.VMEM((shards, 2 * rows, width), jnp.float32),
             pltpu.VMEM((length, width), jnp.bfloat16),
-            pltpu.VMEM((heads, length, HEAD_DIM), jnp.bfloat16),
+            pltpu.VMEM((length, width), jnp.bfloat16),
             pltpu.VMEM((rows, length), jnp.float32),
             pltpu.VMEM((rows, length), jnp.bfloat16),
             pltpu.VMEM((rows, HEAD_DIM), jnp.float32),
+            pltpu.VMEM((2 * rows, 2 * rows), jnp.bfloat16),
+            pltpu.VMEM((2 * rows, 2 * rows), jnp.bfloat16),
+            pltpu.VMEM((rows, 2 * rows), jnp.bfloat16),
+            pltpu.VMEM((rows, 2 * rows), jnp.bfloat16),
+            pltpu.VMEM((1, channels), jnp.float32),
             pltpu.SemaphoreType.DMA((streams,)),
             pltpu.SemaphoreType.DMA((streams, shards)),
             pltpu.SemaphoreType.DMA((streams, shards)),
-            pltpu.SemaphoreType.DMA((1 + heads, shards)),
-            pltpu.SemaphoreType.DMA((1 + heads, shards)),
-            pltpu.SemaphoreType.DMA((2, max(heads, 1))),
+            pltpu.SemaphoreType.DMA((2, shards)),
+            pltpu.SemaphoreType.DMA((2, shards)),
+            pltpu.SemaphoreType.DMA((2,)),
+            pltpu.SemaphoreType.DMA((5,)),
         ],
         compiler_params=pltpu.CompilerParams(
             collective_id=0, has_side_effects=True, vmem_limit_bytes=56 * 1024 * 1024
@@ -550,7 +554,7 @@
         in_specs=[in_place] * 2,
         out_specs=(in_place, in_place),
         scratch_shapes=[pltpu.SemaphoreType.DMA((2, HAND_OVERS))],
-        compiler_params=pltpu.CompilerParams(vmem_limit_bytes=56 * 1024 * 1024),
+        compiler_params=pltpu.CompilerParams(vmem_limit_bytes=4 * 1024 * 1024),
         name="hand_over",
     )(*results)
 
@@ -561,9 +565,9 @@
 def hand_over(first, second, first_out, second_out, sems):
     rows = first.shape[0] // HAND_OVERS
     copies = []
-    for number, (source, target) in enumerate(((first, first_out), (second, second_out))):
-        for part in range(HAND_OVERS):
-            span = pl.ds(part * rows, rows)
+    for part in range(HAND_OVERS):
+        span = pl.ds(part * rows, rows)
+        for number, (source, target) in enumerate(((first, first_out), (second, second_out))):
             copies.append(pltpu.make_async_copy(source.at[span, :], target.at[span, :], sems.at[number, part]))
     for copy in copies:
         copy.start()

time: 153 us -> 93.6 us (0.61)
  Pallas kernels: 152 us -> 92.6 us
    pallas_call x1, Pallas kernels: 64.7 us -> 1.38 us  [by_heads(): pl.pallas_call(hand_over, out_shape=(shape, shape), in_specs=[in_place] *...]
    pallas_call x1, Pallas kernels: 87.2 us -> 91.2 us  [by_heads(): pl.pallas_call(functools.partial(fused_kernel, shards), out_shape=(landin...]
where the time goes in v5:
time: 93.6 us; the launch traced here: 93.2 us
  Pallas kernels  92.6 us (99%)
    pallas_call x1, Pallas kernels, by_heads(): pl.pallas_call(functools.partial(fused_kernel, shards), out_shape=(landin...  91.2 us

profile of v5, /device:TPU:0, one launch (start us, length us, event | category | flops | bytes accessed | tf_op | source)
XLA Modules:
  0.0 93.2 jit_solution(2878236916497178645)
XLA Ops:
  0.6 91.2 %conv_attention.1 = (bf16[256,2048]{1,0:T(8,128)(2,1)S(1)}, bf16[256,2048]{1,0:T(8,128)(2,1)S(1)}) custom-call(bf16[512,512]{1,0:T(8,128)(2,1)} %constant.8.clone.fwd_hi_in, bf16[512,512]{1,0:T(8,128)(2,1)} %constant.9.clone.fwd_lo_in, bf16[256,512]{1,0:T(8,128)(2,1)} %constant.10.clone.inv_hi_in, bf16[256,512]{1,0:T(8,128)(2,1)} %constant.11.clone.inv_lo_in, ...), custom_call_target="tpu_custom_call" | custom-call | tf_op jit(solution)/shard_map/conv_attention/pallas_call | solution.py:509
  91.9 1.4 %hand_over.1 = (bf16[256,2048]{1,0:T(8,128)(2,1)}, bf16[256,2048]{1,0:T(8,128)(2,1)}) custom-call(bf16[256,2048]{1,0:T(8,128)(2,1)S(1)} %get-tuple-element.4.first, bf16[256,2048]{1,0:T(8,128)(2,1)S(1)} %get-tuple-element.5.second), custom_call_target="tpu_custom_call" | custom-call | tf_op jit(solution)/shard_map/hand_over/pallas_call | solution.py:551

commit v6 on v5

--- a/solution.py
+++ b/solution.py
@@ -311,6 +311,7 @@
     wide_copy.wait()
     taps_sent[...] = taps_wide[...].astype(jnp.bfloat16)
     start_stream(1)
+    start_stream(2)
 
     def spectrum(index):
         signal = v_buf[block(index), :]
@@ -329,7 +330,6 @@
 
     lax.fori_loop(1, shards, signal_step, 0)
 
-    start_stream(2)
     wait_stream(1)
     start_stream(3)
     start_stream(4)
@@ -393,12 +393,23 @@
     def mix_step(turn, carry):
         step = ordered(turn)
         mix(partner(step))
-        mixed_send(step).start()
         return carry
 
     lax.fori_loop(1, shards, mix_step, 0)
     mix(me)
     mixed_own().start()
+
+    def left(step, carry):
+        send(3, step).wait_send()
+        send(4, step).wait_send()
+        return carry
+
+    def return_mixed(turn, carry):
+        mixed_send(ordered(turn)).start()
+        return carry
+
+    lax.fori_loop(1, shards, left, 0)
+    lax.fori_loop(1, shards, return_mixed, 0)
 
     scale = math.log2(math.e) / math.sqrt(HEAD_DIM)
 
@@ -485,7 +496,7 @@
         ).wait_recv()
 
     def finish(step, carry):
-        for stream in range(len(streams)):
+        for stream in range(3):
             send(stream, step).wait_send()
         mixed_send(step).wait_send()
         att_send(step).wait_send()

time: 93.6 us -> 93.3 us (level)
  no operation moved by 1% of the time
where the time goes in v6:
time: 93.3 us; the launch traced here: 93.1 us
  Pallas kernels  92.5 us (99%)
    pallas_call x1, Pallas kernels, by_heads(): pl.pallas_call(functools.partial(fused_kernel, shards), out_shape=(landin...  91.1 us

profile of v6, /device:TPU:0, one launch (start us, length us, event | category | flops | bytes accessed | tf_op | source)
XLA Modules:
  0.0 93.1 jit_solution(4375461525590757424)
XLA Ops:
  0.6 91.1 %conv_attention.1 = (bf16[256,2048]{1,0:T(8,128)(2,1)S(1)}, bf16[256,2048]{1,0:T(8,128)(2,1)S(1)}) custom-call(bf16[512,512]{1,0:T(8,128)(2,1)} %constant.8.clone.fwd_hi_in, bf16[512,512]{1,0:T(8,128)(2,1)} %constant.9.clone.fwd_lo_in, bf16[256,512]{1,0:T(8,128)(2,1)} %constant.10.clone.inv_hi_in, bf16[256,512]{1,0:T(8,128)(2,1)} %constant.11.clone.inv_lo_in, ...), custom_call_target="tpu_custom_call" | custom-call | tf_op jit(solution)/shard_map/conv_attention/pallas_call | solution.py:520
  91.8 1.4 %hand_over.1 = (bf16[256,2048]{1,0:T(8,128)(2,1)}, bf16[256,2048]{1,0:T(8,128)(2,1)}) custom-call(bf16[256,2048]{1,0:T(8,128)(2,1)S(1)} %get-tuple-element.4.first, bf16[256,2048]{1,0:T(8,128)(2,1)S(1)} %get-tuple-element.5.second), custom_call_target="tpu_custom_call" | custom-call | tf_op jit(solution)/shard_map/hand_over/pallas_call | solution.py:562

commit v7 on v6

--- a/solution.py
+++ b/solution.py
@@ -437,29 +437,23 @@
             (((1,), (1,)), ((), ())),
             preferred_element_type=jnp.float32,
         )
-        tile = 16 if reach > 4 * rows else 32
-
-        def softmax_tile(turn, carry):
-            span = pl.ds(pl.multiple_of(turn * tile, tile), tile)
-            row = lax.broadcasted_iota(jnp.int32, (tile, rows), 0) + turn * tile
-            column = lax.broadcasted_iota(jnp.int32, (tile, rows), 1)
-            last = jnp.where(column <= row, s_buf[span, before:reach], -1e30)
-            highest = jnp.max(last, axis=1, keepdims=True)
-            if index:
-                early = s_buf[span, 0:before]
-                highest = jnp.maximum(highest, jnp.max(early, axis=1, keepdims=True))
-            top = highest * scale
-            last = jnp.exp2(last * scale - top)
-            total = jnp.sum(last, axis=1, keepdims=True)
-            p_buf[span, before:reach] = last.astype(jnp.bfloat16)
-            if index:
-                early = jnp.exp2(early * scale - top)
-                total += jnp.sum(early, axis=1, keepdims=True)
-                p_buf[span, 0:before] = early.astype(jnp.bfloat16)
-            l_buf[span, :] = jnp.broadcast_to(total, (tile, HEAD_DIM))
-            return carry
-
-        lax.fori_loop(0, rows // tile, softmax_tile, 0, unroll=2)
+        row = lax.broadcasted_iota(jnp.int32, (rows, rows), 0)
+        column = lax.broadcasted_iota(jnp.int32, (rows, rows), 1)
+        s_buf[:, before:reach] = jnp.where(column <= row, s_buf[:, before:reach], -1e30)
+        highest = s_buf[:, 0:LANES]
+        for lane in range(LANES, reach, LANES):
+            highest = jnp.maximum(highest, s_buf[:, lane : lane + LANES])
+        l_buf[...] = jnp.broadcast_to(jnp.max(highest, axis=1, keepdims=True) * scale, (rows, LANES))
+        tile = rows // 2
+        for start in range(0, rows, tile):
+            span = slice(start, start + tile)
+            top = l_buf[span, :]
+            total = jnp.zeros((tile, LANES), jnp.float32)
+            for lane in range(0, reach, LANES):
+                weights = jnp.exp2(s_buf[span, lane : lane + LANES] * scale - top)
+                total += weights
+                p_buf[span, lane : lane + LANES] = weights.astype(jnp.bfloat16)
+            l_buf[span, :] = jnp.broadcast_to(jnp.sum(total, axis=1, keepdims=True), (tile, LANES))
         update = dot32(p_buf[:, 0:reach], m_buf[0:reach, part])
         a_buf[before:reach, part] = (update / l_buf[...]).astype(jnp.bfloat16)
 

time: 93.3 us -> 87.5 us (0.938)
  Pallas kernels: 92.5 us -> 86.5 us
    pallas_call x1, Pallas kernels: 91.1 us -> 85.1 us  [by_heads(): pl.pallas_call(functools.partial(fused_kernel, shards), out_shape=(landin...]
where the time goes in v7:
time: 87.5 us; the launch traced here: 87.1 us
  Pallas kernels  86.5 us (99%)
    pallas_call x1, Pallas kernels, by_heads(): pl.pallas_call(functools.partial(fused_kernel, shards), out_shape=(landin...  85.1 us

profile of v7, /device:TPU:0, one launch (start us, length us, event | category | flops | bytes accessed | tf_op | source)
XLA Modules:
  0.0 87.1 jit_solution(14111108052878973675)
XLA Ops:
  0.6 85.1 %conv_attention.1 = (bf16[256,2048]{1,0:T(8,128)(2,1)S(1)}, bf16[256,2048]{1,0:T(8,128)(2,1)S(1)}) custom-call(bf16[512,512]{1,0:T(8,128)(2,1)} %constant.8.clone.fwd_hi_in, bf16[512,512]{1,0:T(8,128)(2,1)} %constant.9.clone.fwd_lo_in, bf16[256,512]{1,0:T(8,128)(2,1)} %constant.10.clone.inv_hi_in, bf16[256,512]{1,0:T(8,128)(2,1)} %constant.11.clone.inv_lo_in, ...), custom_call_target="tpu_custom_call" | custom-call | tf_op jit(solution)/shard_map/conv_attention/pallas_call | solution.py:514
  85.7 1.4 %hand_over.1 = (bf16[256,2048]{1,0:T(8,128)(2,1)}, bf16[256,2048]{1,0:T(8,128)(2,1)}) custom-call(bf16[256,2048]{1,0:T(8,128)(2,1)S(1)} %get-tuple-element.4.first, bf16[256,2048]{1,0:T(8,128)(2,1)S(1)} %get-tuple-element.5.second), custom_call_target="tpu_custom_call" | custom-call | tf_op jit(solution)/shard_map/hand_over/pallas_call | solution.py:556
